TPU v7x, 32 devices: a whole 2x2x4 slice. The times are simulated.
32 devices in a mesh: dp: 8 (over z, y), tensor: 4 (over x, core).
Axes of the slice: x: 2, y: 2, z: 4, core: 2. Of those that a mesh axis runs over, the one named last changes fastest.
Arguments:
- tokens: bfloat16 [16384, 768], P(('dp', 'tensor')), may hold values from -6 to 6
- lengths: int32 [16, 8], P('dp'), may hold values from 1 to 256, 1024 in all within a row
- cotangent: bfloat16 [16384, 768], P(('dp', 'tensor')), may hold values from -6 to 6
- query_weight: bfloat16 [768, 768], P(None, 'tensor'), may hold values from -0.21875 to 0.21875
- query_bias: float32 [768], P('tensor'), may hold values from -3 to 3
- key_weight: bfloat16 [768, 768], P(None, 'tensor'), may hold values from -0.21875 to 0.21875
- value_weight: bfloat16 [768, 768], P(None, 'tensor'), may hold values from -0.21875 to 0.21875
- value_bias: float32 [768], P('tensor'), may hold values from -3 to 3
- out_weight: bfloat16 [768, 768], P('tensor'), may hold values from -1.25 to 1.25
- out_bias: float32 [768], replicated, may hold values from -3 to 3
- gain_one: float32 [768], replicated, may hold values from 0.25 to 1.75
- shift_one: float32 [768], replicated, may hold values from -3 to 3
- up_weight: bfloat16 [768, 3072], P(None, 'tensor'), may hold values from -0.21875 to 0.21875
- up_bias: float32 [3072], P('tensor'), may hold values from -3 to 3
- down_weight: bfloat16 [3072, 768], P('tensor'), may hold values from -0.109375 to 0.109375
- down_bias: float32 [768], replicated, may hold values from -3 to 3
- gain_two: float32 [768], replicated, may hold values from 0.25 to 1.75
- shift_two: float32 [768], replicated, may hold values from -3 to 3
Outputs:
- layer_output: bfloat16 [16384, 768], P(('dp', 'tensor'))
- tokens_grad: float32 [16384, 768], P(('dp', 'tensor'))
- query_weight_grad: float32 [768, 768], P(None, 'tensor')
- query_bias_grad: float32 [768], P('tensor')
- key_weight_grad: float32 [768, 768], P(None, 'tensor')
- value_weight_grad: float32 [768, 768], P(None, 'tensor')
- value_bias_grad: float32 [768], P('tensor')
- out_weight_grad: float32 [768, 768], P('tensor')
- out_bias_grad: float32 [768], replicated
- gain_one_grad: float32 [768], replicated
- shift_one_grad: float32 [768], replicated
- up_weight_grad: float32 [768, 3072], P(None, 'tensor')
- up_bias_grad: float32 [3072], P('tensor')
- down_weight_grad: float32 [3072, 768], P('tensor')
- down_bias_grad: float32 [768], replicated
- gain_two_grad: float32 [768], replicated
- shift_two_grad: float32 [768], replicated
Inputs may be any that keep to these rules, and one draw needn't show every extreme that they name: Each row of lengths sums to 1024, and its largest entry is 256.
All inputs are finite; a program needn't handle non-finite values.
Results may differ from a plain program's by a relative error of at most 0.02.
Values may be sent and summed in bfloat16 or wider, within the bound.
No kernel may reach another device: no remote copies, remote signals or barrier semaphores. Data moves between devices by JAX's collectives and lax.ppermute only.
A program may use at most 128 MiB of HBM per device.

v0:
```python
import jax
import jax.numpy as jnp
from jax import lax
from jax.sharding import PartitionSpec as P

HEAD_DIM = 64


EPSILON = 1e-05
MASKED = -1e30


def product(left_side, right_side):
    return jnp.dot(left_side, right_side, preferred_element_type=jnp.float32)


def rows_product(left_side, right_side):
    return lax.dot_general(
        left_side, right_side, (((0,), (0,)), ((), ())), preferred_element_type=jnp.float32
    )


def cols_product(left_side, right_side):
    return lax.dot_general(
        left_side, right_side, (((1,), (1,)), ((), ())), preferred_element_type=jnp.float32
    )


def norm_forward(values_in, gain, shift):
    row_mean = jnp.mean(values_in, axis=-1, keepdims=True)
    centered = values_in - row_mean
    row_var = jnp.mean(centered * centered, axis=-1, keepdims=True)
    inverse = lax.rsqrt(row_var + EPSILON)
    normal = centered * inverse
    return (normal * gain + shift, normal, inverse)


def norm_backward(upstream, normal, inverse, gain):
    scaled = upstream * gain
    first_mean = jnp.mean(scaled, axis=-1, keepdims=True)
    second_mean = jnp.mean(scaled * normal, axis=-1, keepdims=True)
    grad_in = inverse * (scaled - first_mean - normal * second_mean)
    return (grad_in, jnp.sum(upstream * normal, axis=0), jnp.sum(upstream, axis=0))


def doc_mask(lengths, row_count):
    doc_ends = jnp.cumsum(lengths)
    places = jnp.arange(row_count, dtype=jnp.int32)
    segment = jnp.sum((places[:, None] >= doc_ends[None, :]).astype(jnp.int32), axis=1)
    return segment[:, None] == segment[None, :]


def masked_scores(queries, key_rows, lengths, score_scale):
    scores = (
        jnp.einsum("qhd,khd->hqk", queries, key_rows, preferred_element_type=jnp.float32)
        * score_scale
    )
    return jnp.where(doc_mask(lengths, queries.shape[0])[None], scores, MASKED)


def attend_one(members, score_scale):
    queries, key_rows, value_rows, lengths = members
    scores = masked_scores(queries, key_rows, lengths, score_scale)
    row_top = jnp.max(scores, axis=-1, keepdims=True)
    weights = jnp.exp(scores - row_top)
    row_total = jnp.sum(weights, axis=-1, keepdims=True)
    low_probs = (weights / row_total).astype(jnp.bfloat16)
    context = jnp.einsum("hqk,khd->qhd", low_probs, value_rows, preferred_element_type=jnp.float32)
    return (context.astype(jnp.bfloat16), (row_top + jnp.log(row_total))[..., 0])


def attend_back_one(members, score_scale):
    queries, key_rows, value_rows, lengths, log_total, grad_context = members
    scores = masked_scores(queries, key_rows, lengths, score_scale)
    prob_rows = jnp.exp(scores - log_total[..., None])
    grad_values = jnp.einsum(
        "hqk,qhd->khd",
        prob_rows.astype(jnp.bfloat16),
        grad_context,
        preferred_element_type=jnp.float32,
    )
    grad_probs = jnp.einsum(
        "qhd,khd->hqk", grad_context, value_rows, preferred_element_type=jnp.float32
    )
    inner_sum = jnp.sum(prob_rows * grad_probs, axis=-1, keepdims=True)
    grad_scores = (prob_rows * (grad_probs - inner_sum)).astype(jnp.bfloat16)
    grad_queries = (
        jnp.einsum("hqk,khd->qhd", grad_scores, key_rows, preferred_element_type=jnp.float32)
        * score_scale
    )
    grad_keys = (
        jnp.einsum("hqk,qhd->khd", grad_scores, queries, preferred_element_type=jnp.float32)
        * score_scale
    )
    return (
        grad_queries.astype(jnp.bfloat16),
        grad_keys.astype(jnp.bfloat16),
        grad_values.astype(jnp.bfloat16),
    )


def body(
    tokens,
    lengths,
    cotangent,
    query_weight,
    query_bias,
    key_weight,
    value_weight,
    value_bias,
    out_weight,
    out_bias,
    gain_one,
    shift_one,
    up_weight,
    up_bias,
    down_weight,
    down_bias,
    gain_two,
    shift_two,
):
    seq_count = lengths.shape[0]
    local_width = query_weight.shape[1]
    score_scale = HEAD_DIM ** (-0.5)

    def to_heads(values_in):
        return values_in.reshape(seq_count, -1, local_width // HEAD_DIM, HEAD_DIM)

    def attention_forward(inputs_full):
        queries = to_heads((product(inputs_full, query_weight) + query_bias).astype(jnp.bfloat16))
        key_rows = to_heads(product(inputs_full, key_weight).astype(jnp.bfloat16))
        value_rows = to_heads(
            (product(inputs_full, value_weight) + value_bias).astype(jnp.bfloat16)
        )
        context, log_total = lax.map(
            lambda members: attend_one(members, score_scale),
            (queries, key_rows, value_rows, lengths),
        )
        return (queries, key_rows, value_rows, context.reshape(-1, local_width), log_total)

    def feed_forward(hidden_full):
        pre_up = product(hidden_full, up_weight) + up_bias
        return (pre_up, jax.nn.gelu(pre_up, approximate=False).astype(jnp.bfloat16))

    inputs_full = lax.all_gather(tokens, "tensor", axis=0, tiled=True)
    queries, key_rows, value_rows, context, log_total = attention_forward(inputs_full)
    attended = lax.psum_scatter(
        product(context, out_weight).astype(jnp.bfloat16), "tensor", scatter_dimension=0, tiled=True
    ).astype(jnp.float32)
    hidden, normal_one, inverse_one = norm_forward(
        tokens.astype(jnp.float32) + attended + out_bias, gain_one, shift_one
    )
    hidden_full = lax.all_gather(hidden.astype(jnp.bfloat16), "tensor", axis=0, tiled=True)
    pre_up, active = feed_forward(hidden_full)
    branch = lax.psum_scatter(
        product(active, down_weight).astype(jnp.bfloat16), "tensor", scatter_dimension=0, tiled=True
    ).astype(jnp.float32)
    layer_output, normal_two, inverse_two = norm_forward(
        hidden + branch + down_bias, gain_two, shift_two
    )
    grad_two, gain_two_grad, shift_two_grad = norm_backward(
        cotangent.astype(jnp.float32), normal_two, inverse_two, gain_two
    )
    down_bias_grad = jnp.sum(grad_two, axis=0)
    hidden_full = lax.all_gather(hidden.astype(jnp.bfloat16), "tensor", axis=0, tiled=True)
    pre_up, active = feed_forward(hidden_full)
    grad_branch = lax.all_gather(grad_two.astype(jnp.bfloat16), "tensor", axis=0, tiled=True)
    down_weight_grad = rows_product(active, grad_branch)
    grad_active = cols_product(grad_branch, down_weight)
    unused, pullback = jax.vjp(lambda inner: jax.nn.gelu(inner, approximate=False), pre_up)
    grad_pre = pullback(grad_active)[0].astype(jnp.bfloat16)
    up_bias_grad = jnp.sum(grad_pre, axis=0, dtype=jnp.float32)
    up_weight_grad = rows_product(hidden_full, grad_pre)
    grad_hidden = grad_two + lax.psum_scatter(
        cols_product(grad_pre, up_weight).astype(jnp.bfloat16),
        "tensor",
        scatter_dimension=0,
        tiled=True,
    ).astype(jnp.float32)
    grad_one, gain_one_grad, shift_one_grad = norm_backward(
        grad_hidden, normal_one, inverse_one, gain_one
    )
    out_bias_grad = jnp.sum(grad_one, axis=0)
    inputs_full = lax.all_gather(tokens, "tensor", axis=0, tiled=True)
    queries, key_rows, value_rows, context, log_total = attention_forward(inputs_full)
    grad_attended = lax.all_gather(grad_one.astype(jnp.bfloat16), "tensor", axis=0, tiled=True)
    out_weight_grad = rows_product(context, grad_attended)
    grad_context = cols_product(grad_attended, out_weight).astype(jnp.bfloat16)
    grad_queries, grad_keys, grad_values = lax.map(
        lambda members: attend_back_one(members, score_scale),
        (queries, key_rows, value_rows, lengths, log_total, to_heads(grad_context)),
    )
    grad_queries = grad_queries.reshape(-1, local_width)
    grad_keys = grad_keys.reshape(-1, local_width)
    grad_values = grad_values.reshape(-1, local_width)
    query_bias_grad = jnp.sum(grad_queries, axis=0, dtype=jnp.float32)
    value_bias_grad = jnp.sum(grad_values, axis=0, dtype=jnp.float32)
    query_weight_grad = rows_product(inputs_full, grad_queries)
    key_weight_grad = rows_product(inputs_full, grad_keys)
    value_weight_grad = rows_product(inputs_full, grad_values)
    partial_sum = cols_product(grad_queries, query_weight)
    partial_sum = partial_sum + cols_product(grad_keys, key_weight)
    tokens_grad = grad_one + lax.psum_scatter(
        (partial_sum + cols_product(grad_values, value_weight)).astype(jnp.bfloat16),
        "tensor",
        scatter_dimension=0,
        tiled=True,
    ).astype(jnp.float32)
    (
        query_weight_grad,
        query_bias_grad,
        key_weight_grad,
        value_weight_grad,
        value_bias_grad,
        out_weight_grad,
        up_weight_grad,
        up_bias_grad,
        down_weight_grad,
    ) = lax.psum(
        (
            query_weight_grad,
            query_bias_grad,
            key_weight_grad,
            value_weight_grad,
            value_bias_grad,
            out_weight_grad,
            up_weight_grad,
            up_bias_grad,
            down_weight_grad,
        ),
        "dp",
    )
    out_bias_grad, gain_one_grad, shift_one_grad, down_bias_grad, gain_two_grad, shift_two_grad = (
        lax.psum(
            (
                out_bias_grad,
                gain_one_grad,
                shift_one_grad,
                down_bias_grad,
                gain_two_grad,
                shift_two_grad,
            ),
            ("dp", "tensor"),
        )
    )
    return (
        layer_output.astype(jnp.bfloat16),
        tokens_grad,
        query_weight_grad,
        query_bias_grad,
        key_weight_grad,
        value_weight_grad,
        value_bias_grad,
        out_weight_grad,
        out_bias_grad,
        gain_one_grad,
        shift_one_grad,
        up_weight_grad,
        up_bias_grad,
        down_weight_grad,
        down_bias_grad,
        gain_two_grad,
        shift_two_grad,
    )


def solution(mesh):
    placed = (
        P(("dp", "tensor"), None),
        P("dp", None),
        P(("dp", "tensor"), None),
        P(None, "tensor"),
        P("tensor"),
        P(None, "tensor"),
        P(None, "tensor"),
        P("tensor"),
        P("tensor", None),
        P(),
        P(),
        P(),
        P(None, "tensor"),
        P("tensor"),
        P("tensor", None),
        P(),
        P(),
        P(),
    )
    return jax.shard_map(
        body,
        mesh=mesh,
        in_specs=placed,
        out_specs=(
            P(("dp", "tensor"), None),
            P(("dp", "tensor"), None),
            P(None, "tensor"),
            P("tensor"),
            P(None, "tensor"),
            P(None, "tensor"),
            P("tensor"),
            P("tensor", None),
            P(),
            P(),
            P(),
            P(None, "tensor"),
            P("tensor"),
            P("tensor", None),
            P(),
            P(),
            P(),
        ),
        check_vma=False,
    )
```

profile of v0, /device:TPU:0, one launch (start us, length us, event | category | flops | bytes accessed | tf_op | source)
XLA Modules:
  0.0 748.7 jit_solution(11029876368825674152)
XLA Ops:
  8.0 32.9 %all-gather.5.cloned.1.call-done = bf16[2048,768]{1,0:T(8,128)(2,1)} async-done(((bf16[512,768]{1,0:T(8,128)(2,1)}), bf16[2048,768]{1,0:T(8,128)(2,1)}) %all-gather.5.cloned.1.call-update) | async-done | bytes 3145744 | tf_op jit(solution)/shard_map/all_gather | solution.py:145
  55.5 35.2 %while.36 = (s32[]{:T(128)}, bf16[2,1024,3,64]{1,3,2,0:T(8,128)(2,1)}, bf16[2,1024,3,64]{1,3,2,0:T(8,128)(2,1)S(1)}, s32[2,8]{1,0:T(2,128)S(1)}, bf16[2,1024,3,6...) while((s32[]{:T(128)}, bf16[2,1024,3,64]{1,3,2,0:T(8,128)(2,1)}, ...), condition=%wide.region_5.6_spmd, body=%wide.region_0.5_spmd.sunk | while | flops 825450560 | bytes 28875012 | solution.py:135
  57.4 9.1 %fusion.204 = (f32[3,1024]{1,0:T(4,128)}, f32[3,1024,1024]{1,2,0:T(8,128)}) fusion(pred[1024,1024]{0,1:T(8,128)(4,1)} %broadcast_compare_fusion.6, bf16[2,1024,3,64]{1,3,2,0:T(8,128)(2,1)S(1)} %get-tuple-element.480, s32[]{:T(128)S(6)} %copy.108, bf16[2,1024,3,64]{1,3,2,0:T(8,128)(2,1)S(1)} %get-tuple-element.479), kind=kOutput, calls=%fused_computation.177.clone.1 | convolution fusion | flops 415237120 | bytes 14431232 | tf_op jit(solution)/shard_map/while/body/eval_jaxpr/sub | solution.py:65
  75.0 9.1 %fusion.204 = (f32[3,1024]{1,0:T(4,128)}, f32[3,1024,1024]{1,2,0:T(8,128)}) fusion(pred[1024,1024]{0,1:T(8,128)(4,1)} %broadcast_compare_fusion.6, bf16[2,1024,3,64]{1,3,2,0:T(8,128)(2,1)S(1)} %get-tuple-element.480, s32[]{:T(128)S(6)} %copy.108, bf16[2,1024,3,64]{1,3,2,0:T(8,128)(2,1)S(1)} %get-tuple-element.479), kind=kOutput, calls=%fused_computation.177.clone.1 | convolution fusion | flops 415237120 | bytes 14431232 | tf_op jit(solution)/shard_map/while/body/eval_jaxpr/sub | solution.py:65
  97.4 37.9 %reduce-scatter.5.cloned.1.call-done = bf16[512,768]{1,0:T(8,128)(2,1)} async-done(((bf16[2048,768]{1,0:T(8,128)(2,1)}), bf16[512,768]{1,0:T(8,128)(2,1)}) %reduce-scatter.5.cloned.1.call-update) | async-done | bytes 786448 | tf_op jit(solution)/shard_map/reduce_scatter | solution.py:147
  140.9 28.6 %all-gather.7.cloned.1.call-done = bf16[2048,768]{1,0:T(8,128)(2,1)} async-done(((bf16[512,768]{1,0:T(8,128)(2,1)}), bf16[2048,768]{1,0:T(8,128)(2,1)}) %all-gather.7.cloned.1.call-update) | async-done | bytes 3145744 | tf_op jit(solution)/shard_map/all_gather | solution.py:153
  169.6 18.4 %multiply_convert_fusion.1 = (bf16[2048,768]{1,0:T(8,128)(2,1)S(1)}, f32[2048,768]{1,0:T(8,128)}, f32[2048,768]{1,0:T(8,128)}) fusion(f32[768]{0:T(1024)S(1)} %copy-done.43, bf16[2048,768]{1,0:T(8,128)(2,1)} %all-gather.7.cloned.1.call-done, bf16[768,768]{1,0:T(8,128)(2,1)S(1)} %copy-done), kind=kOutput, calls=%fused_computation.111 | convolution fusion | flops 2519728128 | bytes 20057088 | tf_op jit(solution)/shard_map/dot_general | solution.py:14
  193.7 38.1 %reduce-scatter.7.cloned.1.call-done = bf16[512,768]{1,0:T(8,128)(2,1)} async-done(((bf16[2048,768]{1,0:T(8,128)(2,1)}), bf16[512,768]{1,0:T(8,128)(2,1)}) %reduce-scatter.7.cloned.1.call-update) | async-done | bytes 786448 | tf_op jit(solution)/shard_map/reduce_scatter | solution.py:155
  239.7 28.2 %all-gather.9.cloned.1.call-done = bf16[2048,768]{1,0:T(8,128)(2,1)} async-done(((bf16[512,768]{1,0:T(8,128)(2,1)}), bf16[2048,768]{1,0:T(8,128)(2,1)}) %all-gather.9.cloned.1.call-update) | async-done | bytes 3145744 | tf_op jit(solution)/shard_map/all_gather | solution.py:167
  267.9 11.0 %convert_reduce_fusion.3 = (f32[768]{0:T(1024)}, bf16[2048,768]{1,0:T(8,128)(2,1)S(1)}) fusion(f32[2048,768]{1,0:T(8,128)} %get-tuple-element.295, f32[2048,768]{1,0:T(8,128)} %get-tuple-element.303, f32[768]{0:T(1024)} %param.37, bf16[2048,768]{1,0:T(8,128)(2,1)} %all-gather.9.cloned.1.call-done, bf16[768,768]{1,0:T(8,128)(2,1)} %param.38), kind=kOutput, calls=%fused_computation.108 | convolution fusion | flops 2442657024 | bytes 20060160 | tf_op jit(solution)/shard_map/dot_general | solution.py:24
  284.8 38.1 %reduce-scatter.9.cloned.1.call-done = bf16[512,768]{1,0:T(8,128)(2,1)} async-done(((bf16[2048,768]{1,0:T(8,128)(2,1)}), bf16[512,768]{1,0:T(8,128)(2,1)}) %reduce-scatter.9.cloned.1.call-update) | async-done | bytes 786448 | tf_op jit(solution)/shard_map/reduce_scatter | solution.py:174
  330.1 44.7 %while.37 = (s32[]{:T(128)}, bf16[2,1024,3,64]{1,3,2,0:T(8,128)(2,1)S(1)}, f32[2,3,1024]{2,1,0:T(4,128)S(1)}, bf16[2,1024,3,64]{1,3,2,0:T(8,128)(2,1)}, s32[2,8]...) while((s32[]{:T(128)}, ...), condition=%wide.region_22.23_spmd, body=%wide.region_17.22_spmd.sunk | while | flops 844320832 | bytes 46790956 | solution.py:135
  331.1 7.3 fusion.208
  338.4 7.5 fusion.209
  360.6 7.4 fusion.209
  386.5 50.5 %while.38 = (s32[]{:T(128)}, bf16[2,1024,3,64]{1,3,2,0:T(8,128)(2,1)}, bf16[2,1024,3,64]{1,3,2,0:T(8,128)(2,1)}, bf16[2,1024,3,64]{1,3,2,0:T(8,128)(2,1)}, bf16[...) while((s32[]{:T(128)}, ...), condition=%wide.region_27.28_spmd, body=%wide.region_23.27_spmd.sunk | while | flops 2062503936 | bytes 124626432 | solution.py:189
  393.3 7.2 multiply_reduce_fusion.7
  400.5 7.0 multiply_convert_fusion.3
  418.3 7.2 multiply_reduce_fusion.7
  425.5 7.0 multiply_convert_fusion.3
  449.9 7.1 fusion.137
  468.5 40.8 %all-reduce = (f32[768]{0:T(1024)}, f32[768]{0:T(1024)}, f32[768]{0:T(1024)}, f32[768]{0:T(1024)}, f32[768]{0:T(1024)}, /*index=5*/f32[768]{0:T(1024)}) all-reduce(f32[768]{0:T(1024)S(1)} %copy-done.38, f32[768]{0:T(1024)S(1)} %copy-done.35, f32[768]{0:T(1024)S(1)} %copy-done.36, ...), channel_id=1, replica_groups=mesh['dp'=8,'tensor'=4] {'dp','tensor'}, use_global_device_ids=true, to_apply=%region_38.39 | all-reduce | flops 4608 | bytes 36864 | tf_op jit(solution)/shard_map/psum | solution.py:234
  509.8 23.9 %all-reduce.1 = (f32[192]{0:T(256)}, f32[192]{0:T(256)}, f32[768]{0:T(1024)}) all-reduce(f32[192]{0:T(256)S(1)} %reduce_sum.220, f32[192]{0:T(256)S(1)} %reduce_sum.222, f32[768]{0:T(1024)S(1)} %copy-done.40), channel_id=1, replica_groups=mesh['dp'=8,'tensor'=4] {'dp'}, use_global_device_ids=true, to_apply=%region_31.32 | all-reduce | flops 1152 | bytes 9216 | tf_op jit(solution)/shard_map/psum | solution.py:219
  536.1 194.6 %all-reduce.5.cloned.1.call-done = (f32[768,192]{0,1:T(8,128)}, f32[768,192]{0,1:T(8,128)}, f32[768,192]{0,1:T(8,128)}, f32[192,768]{1,0:T(8,128)}, f32[768,768]{1,0:T(8,128)}, /*index=5*/f32[768,768]{1,0:T(8,128)}) async-done(((f32[768,192]{0,1:T(8,128)}, f32[768,192]{0,1:T(8,128)}, f32[768,192]{0,1:T(8,128)}, f32[192,768]{1,0:T(8,128)}, f32[768,768]{1,0:T(8,128)}, /*index=5*/f32[768,768]{1,0:T(8,128)}), ...) | async-done | bytes 7077904 | tf_op jit(solution)/shard_map/psum | solution.py:219
  (246 shorter events, 164.6 us)
Async XLA Ops:
  7.2 162.4 %copy-start = (bf16[768,768]{1,0:T(8,128)(2,1)S(1)}, bf16[768,768]{1,0:T(8,128)(2,1)}, u32[]{:S(2)}) copy-start(bf16[768,768]{1,0:T(8,128)(2,1)} %param.36) | copy-start | bytes 3538948
  7.2 33.7 %all-gather.5.cloned.1.call-start = ((), (), s32[]{:S(2)}) async-start(), calls=%async_computation.4 | async-start | bytes 3932160 | tf_op jit(solution)/shard_map/all_gather | solution.py:145
  7.9 127.4 %reduce-scatter.5.cloned.1.call-start = ((), (), s32[]{:S(2)}) async-start(), calls=%async_computation.5 | async-start | bytes 3932160 | tf_op jit(solution)/shard_map/reduce_scatter | solution.py:147
  8.0 36.7 %copy-start.44 = (f32[192]{0:T(256)S(1)}, f32[192]{0:T(256)}, u32[]{:S(2)}) copy-start(f32[192]{0:T(256)} %param.28) | copy-start | bytes 2308
  93.4 41.9 %copy-start.2 = (bf16[512,768]{1,0:T(8,128)(2,1)S(1)}, bf16[512,768]{1,0:T(8,128)(2,1)}, u32[]{:S(2)}) copy-start(bf16[512,768]{1,0:T(8,128)(2,1)} %param.24) | copy-start | bytes 2359300
  93.4 41.9 %copy-start.31 = (f32[768]{0:T(1024)S(1)}, f32[768]{0:T(1024)}, u32[]{:S(2)}) copy-start(f32[768]{0:T(1024)} %param.33) | copy-start | bytes 9220
  97.2 41.2 %copy-start.32 = (f32[768]{0:T(1024)S(1)}, f32[768]{0:T(1024)}, u32[]{:S(2)}) copy-start(f32[768]{0:T(1024)} %param.34) | copy-start | bytes 9220
  97.2 41.2 %copy-start.39 = (f32[768]{0:T(1024)S(1)}, f32[768]{0:T(1024)}, u32[]{:S(2)}) copy-start(f32[768]{0:T(1024)} %param.35) | copy-start | bytes 9220
  97.2 72.4 %copy-start.43 = (f32[768]{0:T(1024)S(1)}, f32[768]{0:T(1024)}, u32[]{:S(2)}) copy-start(f32[768]{0:T(1024)} %param.37) | copy-start | bytes 9220
  97.2 72.4 %all-gather.7.cloned.1.call-start = ((), (), s32[]{:S(2)}) async-start(), calls=%async_computation.6 | async-start | bytes 3932160 | tf_op jit(solution)/shard_map/all_gather | solution.py:153
  140.9 90.9 %reduce-scatter.7.cloned.1.call-start = ((), (), s32[]{:S(2)}) async-start(), calls=%async_computation.7 | async-start | bytes 3932160 | tf_op jit(solution)/shard_map/reduce_scatter | solution.py:155
  169.6 20.1 %copy-start.42 = (bf16[768,768]{1,0:T(8,128)(2,1)S(1)}, bf16[768,768]{1,0:T(8,128)(2,1)}, u32[]{:S(2)}) copy-start(bf16[768,768]{1,0:T(8,128)(2,1)} %param.38) | copy-start | bytes 3538948
  189.7 42.1 %copy-start.4 = (bf16[512,768]{1,0:T(8,128)(2,1)S(1)}, bf16[512,768]{1,0:T(8,128)(2,1)}, u32[]{:S(2)}) copy-start(bf16[512,768]{1,0:T(8,128)(2,1)} %reduce-scatter.5.cloned.1.call-done) | copy-start | bytes 2359300
  193.7 74.3 %all-gather.9.cloned.1.call-start = ((), (), s32[]{:S(2)}) async-start(), calls=%async_computation.8 | async-start | bytes 3932160 | tf_op jit(solution)/shard_map/all_gather | solution.py:167
  239.3 83.6 %reduce-scatter.9.cloned.1.call-start = ((), (), s32[]{:S(2)}) async-start(), calls=%async_computation.9 | async-start | bytes 3932160 | tf_op jit(solution)/shard_map/reduce_scatter | solution.py:174
  284.7 90.2 %all-gather.11.cloned.1.call-start = ((), (), s32[]{:S(2)}) async-start(), calls=%async_computation.10 | async-start | bytes 3932160 | tf_op jit(solution)/shard_map/all_gather | solution.py:186
  329.8 203.9 %reduce-scatter.11.cloned.1.call-start = ((), (), s32[]{:S(2)}) async-start(), calls=%async_computation.11 | async-start | bytes 3932160 | tf_op jit(solution)/shard_map/reduce_scatter | solution.py:203
  338.4 7.5 copy-start.11
  447.4 283.4 %all-reduce.5.cloned.1.call-start = ((), (), s32[]{:S(2)}) async-start(), calls=%async_computation.12 | async-start | bytes 14155776 | tf_op jit(solution)/shard_map/psum | solution.py:219
  467.8 41.5 %copy-start.16 = (bf16[2,1024,3,64]{1,3,2,0:T(8,128)(2,1)S(1)}, bf16[2,1024,3,64]{1,3,2,0:T(8,128)(2,1)}, u32[]{:S(2)}) copy-start(bf16[2,1024,3,64]{1,3,2,0:T(8,128)(2,1)} %get-tuple-element.145) | copy-start | bytes 2359300
  467.8 42.1 %copy-start.40 = (f32[768]{0:T(1024)S(1)}, f32[768]{0:T(1024)}, u32[]{:S(2)}) copy-start(f32[768]{0:T(1024)} %get-tuple-element.288) | copy-start | bytes 9220
  467.8 65.9 %copy-start.8 = (f32[512,768]{1,0:T(8,128)S(1)}, f32[512,768]{1,0:T(8,128)}, u32[]{:S(2)}) copy-start(f32[512,768]{1,0:T(8,128)} %copy-done.7) | copy-start | bytes 4718596
  730.8 8.1 %copy-start.27 = (f32[768,768]{1,0:T(8,128)S(1)}, f32[768,768]{1,0:T(8,128)}, u32[]{:S(2)}) copy-start(f32[768,768]{1,0:T(8,128)} %get-tuple-element.557) | copy-start | bytes 7077892
  732.8 7.4 copy-start.26
  (44 other events, 144.2 us)
Sparse Core Ops, SparseCore 0:
  9.6 31.2 all-gather.4
  97.3 37.9 reduce-scatter.4
  141.0 28.5 all-gather.6
  193.8 37.9 reduce-scatter.6
  239.4 28.5 all-gather.8
  284.9 37.9 reduce-scatter.8
  329.9 28.5 all-gather.10
  447.5 38.8 reduce-scatter.10
  492.7 238.0 all-reduce.4
where the time goes:
time: 757 us; the launch traced here: 749 us
  waiting for transfers between devices  399 us (53%)
  matrix products  168 us (22%)
  blocking collectives  64.7 us (9%)
  other arithmetic  57.8 us (8%)
  local copies, waits for them, and re-layouts  41.5 us (5%)
  between operations  14.8 us (2%)
    psum x1, waiting for transfers between devices, body(): lax.psum((query_weight_grad, query_bias_grad, key_weight_grad, value_weig...  195 us
    psum x1, blocking collectives, body(): lax.psum((out_bias_grad, gain_one_grad, shift_one_grad, down_bias_grad, g...  40.8 us
    reduce_scatter x1, waiting for transfers between devices, body(): lax.psum_scatter(cols_product(grad_pre, up_weight).astype(jnp.bfloat16),...  38.1 us
    reduce_scatter x1, waiting for transfers between devices, body(): lax.psum_scatter(product(active, down_weight).astype(jnp.bfloat16), 'tens...  38.1 us
    reduce_scatter x1, waiting for transfers between devices, body(): lax.psum_scatter(product(context, out_weight).astype(jnp.bfloat16), 'tens...  37.9 us
    dot_general x6, matrix products, product(): return jnp.dot(left_side, right_side, preferred_element_type=jnp.float32)  35.4 us
    all_gather x1, waiting for transfers between devices, body(): inputs_full = lax.all_gather(tokens, 'tensor', axis=0, tiled=True)  32.9 us
    all_gather x1, waiting for transfers between devices, body(): lax.all_gather(hidden.astype(jnp.bfloat16), 'tensor', axis=0, tiled=True)  28.6 us
  transfers between devices with their start and end apart: 9, of which 7 were waited for; matrix products, arithmetic and copies ran while one was open for 9% of the time, Pallas kernels for 0%

commit v1 on v0

v1 whole, which is shorter than its diff:
```python
import functools

import jax
import jax.numpy as jnp
from jax import lax
from jax.experimental import pallas as pl
from jax.experimental.pallas import tpu as pltpu
from jax.sharding import PartitionSpec as P

HEAD_DIM = 64
MOST = 256
EPSILON = 1e-05
MASKED = -1e30
QUERY_BLOCK = 256
UNIT_BLOCK = 256
EXTRA = 64
VMEM_LIMIT = 48 * 1024 * 1024

TAIL_SCALE = 0.425
TAIL = (
    0.23966740682492862,
    0.24201181237516,
    0.19964184258583956,
    0.2585875675603689,
    -0.10985333090134082,
    0.4147788772153898,
    -0.3173079260911745,
    0.07247363954140279,
)

BF16 = jnp.bfloat16
F32 = jnp.float32


def product(left_side, right_side):
    return jnp.dot(left_side, right_side, preferred_element_type=F32)


def rows_product(left_side, right_side):
    return lax.dot_general(
        left_side, right_side, (((0,), (0,)), ((), ())), preferred_element_type=F32
    )


def cols_product(left_side, right_side):
    return lax.dot_general(
        left_side, right_side, (((1,), (1,)), ((), ())), preferred_element_type=F32
    )


def norm_forward(values_in, gain, shift):
    row_mean = jnp.mean(values_in, axis=-1, keepdims=True)
    centered = values_in - row_mean
    row_var = jnp.mean(centered * centered, axis=-1, keepdims=True)
    inverse = lax.rsqrt(row_var + EPSILON)
    normal = centered * inverse
    return (normal * gain + shift, normal, inverse)


def norm_backward(upstream, normal, inverse, gain):
    scaled = upstream * gain
    first_mean = jnp.mean(scaled, axis=-1, keepdims=True)
    second_mean = jnp.mean(scaled * normal, axis=-1, keepdims=True)
    grad_in = inverse * (scaled - first_mean - normal * second_mean)
    return (grad_in, jnp.sum(upstream * normal, axis=0), jnp.sum(upstream, axis=0))


def normal_parts(z):
    size = jnp.abs(z)
    t = 1.0 / (1.0 + (TAIL_SCALE * 0.7071067811865476) * size)
    series = TAIL[-1]
    for factor in TAIL[-2::-1]:
        series = series * t + factor
    bell = jnp.exp(-0.5 * z * z)
    tail = (0.5 * bell) * (series * t)
    return jnp.where(z >= 0.0, 1.0 - tail, tail), bell * 0.3989422804014327


def attend_kernel(q_ref, kv_ref, seg_k_ref, seg_q_ref, context_ref, log_ref):
    width = context_ref.shape[1]
    bias = jnp.where(seg_k_ref[...] == seg_q_ref[...], 0.0, MASKED).astype(F32)
    for h in range(width // HEAD_DIM):
        low, high = h * HEAD_DIM, (h + 1) * HEAD_DIM
        queries = q_ref[:, low:high] * BF16(HEAD_DIM**-0.5)
        key_rows = kv_ref[:, width + low : width + high]
        value_rows = kv_ref[:, 2 * width + low : 2 * width + high]
        scores = cols_product(key_rows, queries) + bias
        top = jnp.max(scores, axis=0, keepdims=True)
        weights = jnp.exp(scores - top)
        total = jnp.sum(weights, axis=0, keepdims=True)
        low_probs = (weights * (1.0 / total)).astype(BF16)
        context = rows_product(value_rows, low_probs)
        context_ref[:, low:high] = context.T.astype(BF16)
        log_ref[h : h + 1, :] = top + jnp.log(total)


def attend(qkv, seg_k, seg_q, own):
    rows, columns = qkv.shape
    width = columns // 3
    heads = width // HEAD_DIM
    block = min(QUERY_BLOCK, own)
    return pl.pallas_call(
        attend_kernel,
        grid=(own // block,),
        in_specs=[
            pl.BlockSpec((block, columns), lambda i: (i, 0)),
            pl.BlockSpec((rows, columns), lambda i: (0, 0)),
            pl.BlockSpec((rows, 1), lambda i: (0, 0)),
            pl.BlockSpec((1, block), lambda i: (0, i)),
        ],
        out_specs=[
            pl.BlockSpec((block, width), lambda i: (i, 0)),
            pl.BlockSpec((8, block), lambda i: (0, i)),
        ],
        out_shape=[
            jax.ShapeDtypeStruct((own, width), BF16),
            jax.ShapeDtypeStruct((8, own), F32),
        ],
        compiler_params=pltpu.CompilerParams(vmem_limit_bytes=VMEM_LIMIT),
        cost_estimate=pl.CostEstimate(
            flops=16 * rows * own * width, bytes_accessed=4 * rows * columns, transcendentals=0
        ),
    )(qkv, qkv, seg_k, seg_q)


def attend_back_kernel(
    q_ref, kv_ref, seg_k_ref, seg_q_ref, log_ref, grad_ref, out_ref, keys_ref, values_ref
):
    step, steps = pl.program_id(0), pl.num_programs(0)
    rows, columns = out_ref.shape
    width = columns // 3
    block = q_ref.shape[0]

    @pl.when(step == 0)
    def start():
        keys_ref[...] = jnp.zeros_like(keys_ref)
        values_ref[...] = jnp.zeros_like(values_ref)
        out_ref[:, :width] = jnp.zeros((rows, width), BF16)

    bias = jnp.where(seg_k_ref[...] == seg_q_ref[...], 0.0, MASKED).astype(F32)
    grad_queries = []
    for h in range(width // HEAD_DIM):
        low, high = h * HEAD_DIM, (h + 1) * HEAD_DIM
        queries = q_ref[:, low:high] * BF16(HEAD_DIM**-0.5)
        key_rows = kv_ref[:, width + low : width + high]
        value_rows = kv_ref[:, 2 * width + low : 2 * width + high]
        grads = grad_ref[:, low:high]
        scores = cols_product(key_rows, queries) + bias
        probs = jnp.exp(scores - log_ref[h : h + 1, :])
        values_ref[:, low:high] += product(probs.astype(BF16), grads)
        grad_probs = cols_product(value_rows, grads)
        inner = jnp.sum(probs * grad_probs, axis=0, keepdims=True)
        grad_scores = (probs * (grad_probs - inner)).astype(BF16)
        keys_ref[:, low:high] += product(grad_scores, queries)
        grad_queries.append(rows_product(key_rows, grad_scores).T)
    here = pl.multiple_of(step * block, block)
    joined = jnp.concatenate(grad_queries, axis=1) * (HEAD_DIM**-0.5)
    out_ref[pl.ds(here, block), :width] = joined.astype(BF16)

    @pl.when(step == steps - 1)
    def finish():
        out_ref[:, width : 2 * width] = keys_ref[...].astype(BF16)
        out_ref[:, 2 * width :] = values_ref[...].astype(BF16)


def attend_back(qkv, seg_k, seg_q, log_total, grad_context, own):
    rows, columns = qkv.shape
    width = columns // 3
    block = min(QUERY_BLOCK, own)
    return pl.pallas_call(
        attend_back_kernel,
        grid=(own // block,),
        in_specs=[
            pl.BlockSpec((block, columns), lambda i: (i, 0)),
            pl.BlockSpec((rows, columns), lambda i: (0, 0)),
            pl.BlockSpec((rows, 1), lambda i: (0, 0)),
            pl.BlockSpec((1, block), lambda i: (0, i)),
            pl.BlockSpec((8, block), lambda i: (0, i)),
            pl.BlockSpec((block, width), lambda i: (i, 0)),
        ],
        out_specs=pl.BlockSpec((rows, columns), lambda i: (0, 0)),
        out_shape=jax.ShapeDtypeStruct((rows, columns), BF16),
        scratch_shapes=[pltpu.VMEM((rows, width), F32), pltpu.VMEM((rows, width), F32)],
        compiler_params=pltpu.CompilerParams(vmem_limit_bytes=VMEM_LIMIT),
        cost_estimate=pl.CostEstimate(
            flops=40 * rows * own * width, bytes_accessed=6 * rows * columns, transcendentals=0
        ),
    )(qkv, qkv, seg_k, seg_q, log_total, grad_context)


def feed_kernel(hidden_ref, up_ref, bias_ref, down_ref, sum_ref, active_ref, slope_ref, out_ref):
    @pl.when(pl.program_id(0) == 0)
    def start():
        out_ref[...] = sum_ref[...]

    pre_up = product(hidden_ref[...], up_ref[...]) + bias_ref[...]
    cumulative, density = normal_parts(pre_up)
    active = (pre_up * cumulative).astype(BF16)
    active_ref[...] = active
    slope_ref[...] = cumulative + pre_up * density
    out_ref[...] += product(active, down_ref[...])


def feed(hidden, up, bias, down, running):
    rows, model = hidden.shape
    units = up.shape[1]
    block = min(UNIT_BLOCK, units)
    return pl.pallas_call(
        feed_kernel,
        grid=(units // block,),
        in_specs=[
            pl.BlockSpec((rows, model), lambda i: (0, 0)),
            pl.BlockSpec((model, block), lambda i: (0, i)),
            pl.BlockSpec((1, block), lambda i: (0, i)),
            pl.BlockSpec((block, model), lambda i: (i, 0)),
            pl.BlockSpec((rows, model), lambda i: (0, 0)),
        ],
        out_specs=[
            pl.BlockSpec((rows, block), lambda i: (0, i)),
            pl.BlockSpec((rows, block), lambda i: (0, i)),
            pl.BlockSpec((rows, model), lambda i: (0, 0)),
        ],
        out_shape=[
            jax.ShapeDtypeStruct((rows, units), BF16),
            jax.ShapeDtypeStruct((rows, units), F32),
            jax.ShapeDtypeStruct((rows, model), F32),
        ],
        compiler_params=pltpu.CompilerParams(vmem_limit_bytes=VMEM_LIMIT),
        cost_estimate=pl.CostEstimate(
            flops=6 * rows * model * units, bytes_accessed=8 * rows * units, transcendentals=0
        ),
    )(hidden, up, bias, down, running)


def body(
    dp_size,
    tokens,
    lengths,
    cotangent,
    query_weight,
    query_bias,
    key_weight,
    value_weight,
    value_bias,
    out_weight,
    out_bias,
    gain_one,
    shift_one,
    up_weight,
    up_bias,
    down_weight,
    down_bias,
    gain_two,
    shift_two,
):
    own, model = tokens.shape
    width = query_weight.shape[1]
    units = up_weight.shape[1]
    place = lax.axis_index("tensor")
    replica = lax.axis_index("dp")
    half_row = place % 2

    def swap_core(values_in):
        return lax.ppermute(values_in, "tensor", [(i, i ^ 1) for i in range(4)])

    def swap_chip(values_in):
        return lax.ppermute(values_in, "tensor", [(i, i ^ 2) for i in range(4)])

    def swap_replica(values_in, bit):
        return lax.ppermute(values_in, "dp", [(i, i ^ (1 << bit)) for i in range(dp_size)])

    def spread(values_in):
        second = swap_core(values_in)
        third = swap_chip(values_in)
        fourth = swap_core(third)
        return (values_in, second, third, fourth)

    halo = swap_core(jnp.where(half_row == 0, tokens[own - MOST :], tokens[:MOST]))
    inputs_full = jnp.concatenate([tokens, halo], axis=0)
    total_rows = own + MOST
    doc_ends = jnp.cumsum(lax.dynamic_index_in_dim(lengths, place // 2, 0, keepdims=False))
    spot = jnp.arange(total_rows, dtype=jnp.int32)
    base = jnp.where(half_row == 0, 0, own)
    halo_base = jnp.where(half_row == 0, own, own - MOST)
    spot = jnp.where(spot < own, base + spot, halo_base + spot - own)
    segment = jnp.sum((spot[:, None] >= doc_ends[None, :]).astype(jnp.int32), axis=1)
    seg_k = segment[:, None]
    seg_q = segment[None, :own]

    biases = jnp.concatenate([query_bias, value_bias, up_bias]).reshape(-1, 128)
    biases = [b.reshape(-1) for b in spread(biases)]
    query_biases = [b[:width] for b in biases]
    value_biases = [b[width : 2 * width] for b in biases]
    up_biases = [b[2 * width :] for b in biases]
    projections = spread(jnp.concatenate([query_weight, key_weight, value_weight], axis=1))
    out_weights = spread(out_weight)
    ups = spread(up_weight)
    downs = spread(down_weight)

    mix_one = tokens.astype(F32) + out_bias
    saved = []
    for j in range(4):
        bias = jnp.concatenate([query_biases[j], jnp.zeros((width,), F32), value_biases[j]])
        qkv = (product(inputs_full, projections[j]) + bias).astype(BF16)
        context, log_total = attend(qkv, seg_k, seg_q, own)
        mix_one = mix_one + product(context, out_weights[j])
        saved.append((qkv, context, log_total))
    hidden, normal_one, inverse_one = norm_forward(mix_one, gain_one, shift_one)
    low_hidden = hidden.astype(BF16)

    mix_two = hidden + down_bias
    actives, slopes = [], []
    for j in range(4):
        active, slope, mix_two = feed(low_hidden, ups[j], up_biases[j][None], downs[j], mix_two)
        actives.append(active)
        slopes.append(slope)
    layer_output, normal_two, inverse_two = norm_forward(mix_two, gain_two, shift_two)
    grad_two, gain_two_grad, shift_two_grad = norm_backward(
        cotangent.astype(F32), normal_two, inverse_two, gain_two
    )
    down_bias_grad = jnp.sum(grad_two, axis=0)
    low_grad_two = grad_two.astype(BF16)

    def reduce_tensor(parts):
        mine = (parts[0].astype(F32) + swap_core(parts[1]).astype(F32)).astype(BF16)
        theirs = (parts[2].astype(F32) + swap_core(parts[3]).astype(F32)).astype(BF16)
        mine = lax.optimization_barrier(mine)
        return (mine.astype(F32) + swap_chip(theirs).astype(F32)).astype(BF16)

    def reduce_replicas(values_in):
        bits = dp_size.bit_length() - 1
        now = values_in
        for bit in range(bits):
            upper = (replica >> bit) & 1
            half = now.shape[0] // 2
            send = lax.dynamic_slice_in_dim(now, (1 - upper) * half, half, 0)
            keep = lax.dynamic_slice_in_dim(now, upper * half, half, 0)
            now = (keep.astype(F32) + swap_replica(send, bit).astype(F32)).astype(BF16)
        for bit in range(bits - 1, -1, -1):
            upper = (replica >> bit) & 1
            other = swap_replica(now, bit)
            now = jnp.where(
                upper == 1,
                jnp.concatenate([other, now], axis=0),
                jnp.concatenate([now, other], axis=0),
            )
        return now.astype(F32)

    grad_hidden = grad_two
    down_grads, up_grads, up_bias_grads = [None] * 4, [None] * 4, [None] * 4
    for j in (1, 3, 2, 0):
        grad_pre = (slopes[j] * cols_product(low_grad_two, downs[j])).astype(BF16)
        down_grads[j] = rows_product(actives[j], low_grad_two).astype(BF16)
        up_grads[j] = rows_product(low_hidden, grad_pre).astype(BF16)
        up_bias_grads[j] = jnp.sum(grad_pre, axis=0, dtype=F32)
        grad_hidden = grad_hidden + cols_product(grad_pre, ups[j])
    down_weight_grad = reduce_replicas(reduce_tensor(down_grads))
    grad_one, gain_one_grad, shift_one_grad = norm_backward(
        grad_hidden, normal_one, inverse_one, gain_one
    )
    out_bias_grad = jnp.sum(grad_one, axis=0)
    low_grad_one = grad_one.astype(BF16)

    out_grads = [rows_product(saved[j][1], low_grad_one).astype(BF16) for j in range(4)]
    packed = [jnp.concatenate([up_grads[j], out_grads[j]], axis=0) for j in range(4)]
    packed = reduce_replicas(reduce_tensor(packed))
    up_weight_grad, out_weight_grad = packed[:model], packed[model:]

    shared = [out_bias_grad, gain_one_grad, shift_one_grad, down_bias_grad, gain_two_grad, shift_two_grad]
    tokens_sum = jnp.zeros((total_rows, model), F32)
    last = [None] * 4
    for j in (1, 3, 2, 0):
        qkv, context, log_total = saved[j]
        grad_context = cols_product(low_grad_one, out_weights[j]).astype(BF16)
        grad_qkv = attend_back(qkv, seg_k, seg_q, log_total, grad_context, own)
        sums = jnp.sum(grad_qkv, axis=0, dtype=F32)
        row = jnp.concatenate(
            [sums[:width], sums[2 * width :], jnp.zeros((model - 2 * width,), F32)]
        )
        extras = jnp.stack(shared + [up_bias_grads[j], row], axis=1).astype(BF16)
        extras = jnp.pad(extras, ((0, 0), (0, EXTRA - extras.shape[1])))
        last[j] = jnp.concatenate(
            [rows_product(inputs_full, grad_qkv).astype(BF16), extras], axis=1
        )
        tokens_sum = tokens_sum + cols_product(grad_qkv, projections[j])
    last = reduce_replicas(reduce_tensor(last))
    from_halo = swap_core(tokens_sum[own:].astype(BF16)).astype(F32)
    tokens_grad = grad_one + tokens_sum[:own]
    blank = jnp.zeros((own - MOST, model), F32)
    tokens_grad = tokens_grad + jnp.where(
        half_row == 0,
        jnp.concatenate([blank, from_halo], axis=0),
        jnp.concatenate([from_halo, blank], axis=0),
    )
    vectors = last[:, 3 * width : 3 * width + 8].T
    return (
        layer_output.astype(BF16),
        tokens_grad,
        last[:, :width],
        vectors[7, :width],
        last[:, width : 2 * width],
        last[:, 2 * width : 3 * width],
        vectors[7, width : 2 * width],
        out_weight_grad,
        vectors[0],
        vectors[1],
        vectors[2],
        up_weight_grad,
        vectors[6],
        down_weight_grad,
        vectors[3],
        vectors[4],
        vectors[5],
    )


def solution(mesh):
    placed = (
        P(("dp", "tensor"), None),
        P("dp", None),
        P(("dp", "tensor"), None),
        P(None, "tensor"),
        P("tensor"),
        P(None, "tensor"),
        P(None, "tensor"),
        P("tensor"),
        P("tensor", None),
        P(),
        P(),
        P(),
        P(None, "tensor"),
        P("tensor"),
        P("tensor", None),
        P(),
        P(),
        P(),
    )
    return jax.shard_map(
        functools.partial(body, mesh.shape["dp"]),
        mesh=mesh,
        in_specs=placed,
        out_specs=(
            P(("dp", "tensor"), None),
            P(("dp", "tensor"), None),
            P(None, "tensor"),
            P("tensor"),
            P(None, "tensor"),
            P(None, "tensor"),
            P("tensor"),
            P("tensor", None),
            P(),
            P(),
            P(),
            P(None, "tensor"),
            P("tensor"),
            P("tensor", None),
            P(),
            P(),
            P(),
        ),
        check_vma=False,
    )
```

time: 757 us -> 431 us (0.57)
  waiting for transfers between devices: 399 us -> 174 us
  matrix products: 168 us -> 70.9 us
  Pallas kernels: 0 us -> 71.1 us
  blocking collectives: 64.7 us -> 0 us
  starting transfers between devices: 1.45 us -> 34.2 us
  other arithmetic: 57.8 us -> 36.9 us
  between operations: 14.8 us -> 2.42 us
    psum x1 -> x0, waiting for transfers between devices: 195 us -> none  [body(): lax.psum((query_weight_grad, query_bias_grad, key_weight_grad, value_weig...]
    ppermute x0 -> x44, waiting for transfers between devices: none -> 174 us  [the longest x8 94.3 us: swap_chip(): return lax.ppermute(values_in, 'tensor', [(i, i ^ 2) for i in range(4)])]
    reduce_scatter x4 -> x0, waiting for transfers between devices: 114 us -> none  [the longest x1 38.1 us: body(): lax.psum_scatter(cols_product(grad_pre, up_weight).astype(jnp.bfloat16),...]
    dot_general x22 -> x8, matrix products: 108 us -> 17.7 us  [product(): return jnp.dot(left_side, right_side, preferred_element_type=F32)]
    all_gather x4 -> x0, waiting for transfers between devices: 89.8 us -> none  [the longest x1 32.9 us: body(): inputs_full = lax.all_gather(tokens, 'tensor', axis=0, tiled=True)]
    pallas_call x0 -> x12, Pallas kernels: none -> 71.1 us  [the longest x4 31 us: feed(): pl.pallas_call(feed_kernel, grid=(units // block,), in_specs=[pl.BlockSpe...]
    psum x2 -> x0, blocking collectives: 64.7 us -> none  [the longest x1 40.8 us: body(): lax.psum((out_bias_grad, gain_one_grad, shift_one_grad, down_bias_grad, g...]
    ppermute x0 -> x44, starting transfers between devices: none -> 34.2 us  [the longest x18 23.4 us: swap_replica(): lax.ppermute(values_in, 'dp', [(i, i ^ 1 << bit) for i in range(dp_size)])]
  transfers between devices with their start and end apart: 9 -> 44, of which waited for: 7 -> 20; matrix products, arithmetic and copies ran while one was open for 9% -> 17% of each run, Pallas kernels for 0% -> 11%
where the time goes in v1:
time: 431 us; the launch traced here: 426 us
  waiting for transfers between devices  174 us (40%)
  Pallas kernels  71.1 us (16%)
  matrix products  70.9 us (16%)
  other arithmetic  36.9 us (9%)
  local copies, waits for them, and re-layouts  36.5 us (8%)
  starting transfers between devices  34.2 us (8%)
    ppermute x8, waiting for transfers between devices, swap_chip(): return lax.ppermute(values_in, 'tensor', [(i, i ^ 2) for i in range(4)])  94.3 us
    ppermute x18, waiting for transfers between devices, swap_replica(): lax.ppermute(values_in, 'dp', [(i, i ^ 1 << bit) for i in range(dp_size)])  77.4 us
    dot_general x16, matrix products, rows_product(): lax.dot_general(left_side, right_side, (((0,), (0,)), ((), ())), preferre...  31.4 us
    pallas_call x4, Pallas kernels, feed(): pl.pallas_call(feed_kernel, grid=(units // block,), in_specs=[pl.BlockSpe...  31 us
    ppermute x18, starting transfers between devices, swap_replica(): lax.ppermute(values_in, 'dp', [(i, i ^ 1 << bit) for i in range(dp_size)])  23.4 us
    unnamed x193, local copies, waits for them, and re-layouts  22.6 us
    pallas_call x4, Pallas kernels, attend_back(): pl.pallas_call(attend_back_kernel, grid=(own // block,), in_specs=[pl.Blo...  22.6 us
    dot_general x16, matrix products, cols_product(): lax.dot_general(left_side, right_side, (((1,), (1,)), ((), ())), preferre...  21.8 us
  transfers between devices with their start and end apart: 44, of which 20 were waited for; matrix products, arithmetic and copies ran while one was open for 17% of the time, Pallas kernels for 11%

profile of v1, /device:TPU:0, one launch (start us, length us, event | category | flops | bytes accessed | tf_op | source)
XLA Modules:
  0.0 426.3 jit_solution(10239830952250119014)
XLA Ops:
  21.5 4.5 %shard_map.305 = (bf16[512,192]{1,0:T(8,128)(2,1)S(1)}, f32[8,512]{1,0:T(8,128)S(1)}) custom-call(bf16[768,576]{1,0:T(8,128)(2,1)S(1)} %add_convert_fusion.12.q_ref.kv_ref, bf16[768,576]{1,0:T(8,128)(2,1)S(1)} %add_convert_fusion.12.q_ref.kv_ref, s32[768,1]{1,0:T(8,128)S(1)} %broadcast_in_dim.18.seg_k_ref, s32[1,512]{1,0:T(1,128)S(1)} %bitcast.113), custom_call_target="tpu_custom_call" | custom-call | flops 1207959552 | bytes 1769472 | tf_op jit(solution)/shard_map/pallas_call | solution.py:102
  51.2 13.2 %collective-permute-done.10.up_ref = bf16[768,768]{1,0:T(8,128)(2,1)S(1)} collective-permute-done((bf16[768,768]{1,0:T(8,128)(2,1)S(1)}, bf16[768,768]{1,0:T(8,128)(2,1)S(1)}, u32[]{:S(2)}, u32[]{:S(2)}) %collective-permute-start.10) | collective-permute-done | bytes 1179680 | tf_op jit(solution)/shard_map/ppermute | solution.py:267
  64.4 24.3 %collective-permute-done.12.down_ref = bf16[768,768]{1,0:T(8,128)(2,1)S(1)} collective-permute-done((bf16[768,768]{1,0:T(8,128)(2,1)S(1)}, bf16[768,768]{1,0:T(8,128)(2,1)S(1)}, u32[]{:S(2)}, u32[]{:S(2)}) %collective-permute-start.12) | collective-permute-done | bytes 1179680 | tf_op jit(solution)/shard_map/ppermute | solution.py:267
  90.5 4.3 %shard_map.308 = (bf16[512,192]{1,0:T(8,128)(2,1)S(1)}, f32[8,512]{1,0:T(8,128)S(1)}) custom-call(bf16[768,576]{1,0:T(8,128)(2,1)S(1)} %add_convert_fusion.9.q_ref.kv_ref, bf16[768,576]{1,0:T(8,128)(2,1)S(1)} %add_convert_fusion.9.q_ref.kv_ref, s32[768,1]{1,0:T(8,128)S(1)} %broadcast_in_dim.18.seg_k_ref, s32[1,512]{1,0:T(1,128)S(1)} %bitcast.116), custom_call_target="tpu_custom_call" | custom-call | flops 1207959552 | bytes 1769472 | tf_op jit(solution)/shard_map/pallas_call | solution.py:102
  99.8 7.5 %shard_map.309 = (bf16[512,768]{1,0:T(8,128)(2,1)S(1)}, f32[512,768]{1,0:T(8,128)S(1)}, f32[512,768]{1,0:T(8,128)}) custom-call(bf16[512,768]{1,0:T(8,128)(2,1)S(1)} %get-tuple-element.85.hidden_ref, bf16[768,768]{1,0:T(8,128)(2,1)S(1)} %copy-done.22, f32[1,768]{1,0:T(1,128)S(1)} %broadcast_in_dim.17.bias_ref, bf16[768,768]{1,0:T(8,128)(2,1)S(1)} %copy-done.6, ...), custom_call_target="tpu_custom_call" | custom-call | flops 1811939328 | bytes 3145728 | tf_op jit(solution)/shard_map/pallas_call | solution.py:208
  108.2 8.3 %shard_map.310 = (bf16[512,768]{1,0:T(8,128)(2,1)S(1)}, f32[512,768]{1,0:T(8,128)S(1)}, f32[512,768]{1,0:T(8,128)}) custom-call(bf16[512,768]{1,0:T(8,128)(2,1)S(1)} %get-tuple-element.85.hidden_ref, bf16[768,768]{1,0:T(8,128)(2,1)S(1)} %collective-permute-done.14.up_ref, f32[1,768]{1,0:T(1,128)S(1)} %bitcast.112, ...), custom_call_target="tpu_custom_call" | custom-call | flops 1811939328 | bytes 3145728 | tf_op jit(solution)/shard_map/pallas_call | solution.py:208
  116.6 7.4 %shard_map.311 = (bf16[512,768]{1,0:T(8,128)(2,1)S(1)}, f32[512,768]{1,0:T(8,128)S(1)}, f32[512,768]{1,0:T(8,128)}) custom-call(bf16[512,768]{1,0:T(8,128)(2,1)S(1)} %get-tuple-element.85.hidden_ref, bf16[768,768]{1,0:T(8,128)(2,1)S(1)} %collective-permute-done.10.up_ref, f32[1,768]{1,0:T(1,128)S(1)} %bitcast.111, ...), custom_call_target="tpu_custom_call" | custom-call | flops 1811939328 | bytes 3145728 | tf_op jit(solution)/shard_map/pallas_call | solution.py:208
  124.0 7.9 %shard_map.312 = (bf16[512,768]{1,0:T(8,128)(2,1)S(1)}, f32[512,768]{1,0:T(8,128)S(1)}, f32[512,768]{1,0:T(8,128)}) custom-call(bf16[512,768]{1,0:T(8,128)(2,1)S(1)} %get-tuple-element.85.hidden_ref, bf16[768,768]{1,0:T(8,128)(2,1)S(1)} %collective-permute-done.11.up_ref, f32[1,768]{1,0:T(1,128)S(1)} %bitcast.110, ...), custom_call_target="tpu_custom_call" | custom-call | flops 1811939328 | bytes 3145728 | tf_op jit(solution)/shard_map/pallas_call | solution.py:208
  171.9 5.5 %shard_map.313 = bf16[768,576]{1,0:T(8,128)(2,1)S(1)} custom-call(bf16[768,576]{1,0:T(8,128)(2,1)S(1)} %copy-done.45, bf16[768,576]{1,0:T(8,128)(2,1)S(1)} %copy-done.45, s32[768,1]{1,0:T(8,128)S(1)} %copy-done.19, s32[1,512]{1,0:T(1,128)S(1)} %bitcast.117, f32[8,512]{1,0:T(8,128)S(1)} %get-tuple-element.49.log_ref, bf16[512,192]{1,0:T(8,128)(2,1)S(1)} %copy.84.grad_ref), custom_call_target="tpu_custom_call" | custom-call | flops 3019898880 | bytes 2654208 | tf_op jit(solution)/shard_map/pallas_call | solution.py:170
  182.1 5.5 %shard_map.316 = bf16[768,576]{1,0:T(8,128)(2,1)S(1)} custom-call(bf16[768,576]{1,0:T(8,128)(2,1)S(1)} %copy-done.43, bf16[768,576]{1,0:T(8,128)(2,1)S(1)} %copy-done.43, s32[768,1]{1,0:T(8,128)S(1)} %copy-done.19, s32[1,512]{1,0:T(1,128)S(1)} %bitcast.118, f32[8,512]{1,0:T(8,128)S(1)} %get-tuple-element.52.log_ref, bf16[512,192]{1,0:T(8,128)(2,1)S(1)} %copy.90.grad_ref), custom_call_target="tpu_custom_call" | custom-call | flops 3019898880 | bytes 2654208 | tf_op jit(solution)/shard_map/pallas_call | solution.py:170
  194.5 5.7 %shard_map.314 = bf16[768,576]{1,0:T(8,128)(2,1)S(1)} custom-call(bf16[768,576]{1,0:T(8,128)(2,1)S(1)} %copy-done.47, bf16[768,576]{1,0:T(8,128)(2,1)S(1)} %copy-done.47, s32[768,1]{1,0:T(8,128)S(1)} %copy-done.19, s32[1,512]{1,0:T(1,128)S(1)} %bitcast.119, f32[8,512]{1,0:T(8,128)S(1)} %get-tuple-element.50.log_ref, bf16[512,192]{1,0:T(8,128)(2,1)S(1)} %copy-done.21), custom_call_target="tpu_custom_call" | custom-call | flops 3019898880 | bytes 2654208 | tf_op jit(solution)/shard_map/pallas_call | solution.py:170
  220.4 5.8 %shard_map.315 = bf16[768,576]{1,0:T(8,128)(2,1)S(1)} custom-call(bf16[768,576]{1,0:T(8,128)(2,1)S(1)} %copy-done.41, bf16[768,576]{1,0:T(8,128)(2,1)S(1)} %copy-done.41, s32[768,1]{1,0:T(8,128)S(1)} %copy-done.19, s32[1,512]{1,0:T(1,128)S(1)} %bitcast.120, f32[8,512]{1,0:T(8,128)S(1)} %get-tuple-element.51.log_ref, bf16[512,192]{1,0:T(8,128)(2,1)S(1)} %copy-done.20), custom_call_target="tpu_custom_call" | custom-call | flops 3019898880 | bytes 2654208 | tf_op jit(solution)/shard_map/pallas_call | solution.py:170
  252.2 16.9 %collective-permute-done.19 = bf16[768,640]{0,1:T(8,128)(2,1)S(1)} collective-permute-done((bf16[768,640]{0,1:T(8,128)(2,1)S(1)}, bf16[768,640]{0,1:T(8,128)(2,1)S(1)}, u32[]{:S(2)}, u32[]{:S(2)}) %collective-permute-start.19) | collective-permute-done | bytes 983072 | tf_op jit(solution)/shard_map/ppermute | solution.py:267
  273.6 7.4 %collective-permute-done.20 = bf16[384,640]{0,1:T(8,128)(2,1)S(1)} collective-permute-done((bf16[384,640]{0,1:T(8,128)(2,1)S(1)}, bf16[384,640]{0,1:T(8,128)(2,1)S(1)}, u32[]{:S(2)}, u32[]{:S(2)}) %collective-permute-start.20) | collective-permute-done | bytes 491552 | tf_op jit(solution)/shard_map/ppermute | solution.py:270
  283.2 11.2 %collective-permute-done.37 = bf16[768,768]{1,0:T(8,128)(2,1)S(1)} collective-permute-done((bf16[768,768]{1,0:T(8,128)(2,1)S(1)}, bf16[768,768]{1,0:T(8,128)(2,1)S(1)}, u32[]{:S(2)}, u32[]{:S(2)}) %collective-permute-start.37) | collective-permute-done | bytes 1179680 | tf_op jit(solution)/shard_map/ppermute | solution.py:267
  300.6 24.5 %collective-permute-done.28 = bf16[960,768]{1,0:T(8,128)(2,1)S(1)} collective-permute-done((bf16[960,768]{1,0:T(8,128)(2,1)S(1)}, bf16[960,768]{1,0:T(8,128)(2,1)S(1)}, u32[]{:S(2)}, u32[]{:S(2)}) %collective-permute-start.28) | collective-permute-done | bytes 1474592 | tf_op jit(solution)/shard_map/ppermute | solution.py:267
  339.7 4.7 %collective-permute-done.29 = bf16[480,768]{1,0:T(8,128)(2,1)} collective-permute-done((bf16[480,768]{1,0:T(8,128)(2,1)}, bf16[480,768]{1,0:T(8,128)(2,1)}, u32[]{:S(2)}, u32[]{:S(2)}) %collective-permute-start.29) | collective-permute-done | bytes 737312 | tf_op jit(solution)/shard_map/ppermute | solution.py:270
  352.5 8.4 %collective-permute-done.30 = bf16[240,768]{1,0:T(8,128)(2,1)S(1)} collective-permute-done((bf16[240,768]{1,0:T(8,128)(2,1)S(1)}, bf16[240,768]{1,0:T(8,128)(2,1)S(1)}, u32[]{:S(2)}, u32[]{:S(2)}) %collective-permute-start.30) | collective-permute-done | bytes 368672 | tf_op jit(solution)/shard_map/ppermute | solution.py:270
  364.1 11.1 %collective-permute-done.31 = bf16[120,768]{1,0:T(8,128)(2,1)S(1)} collective-permute-done((bf16[120,768]{1,0:T(8,128)(2,1)S(1)}, bf16[120,768]{1,0:T(8,128)(2,1)S(1)}, u32[]{:S(2)}, u32[]{:S(2)}) %collective-permute-start.31) | collective-permute-done | bytes 184352 | tf_op jit(solution)/shard_map/ppermute | solution.py:270
  381.1 4.6 %collective-permute-done.32 = bf16[120,768]{1,0:T(8,128)(2,1)S(1)} collective-permute-done((bf16[120,768]{1,0:T(8,128)(2,1)S(1)}, bf16[120,768]{1,0:T(8,128)(2,1)S(1)}, u32[]{:S(2)}, u32[]{:S(2)}) %collective-permute-start.32) | collective-permute-done | bytes 184352 | tf_op jit(solution)/shard_map/ppermute | solution.py:270
  386.1 5.9 %collective-permute-done.42 = bf16[192,768]{1,0:T(8,128)(2,1)S(1)} collective-permute-done((bf16[192,768]{1,0:T(8,128)(2,1)S(1)}, bf16[192,768]{1,0:T(8,128)(2,1)S(1)}, u32[]{:S(2)}, u32[]{:S(2)}) %collective-permute-start.42) | collective-permute-done | bytes 294944 | tf_op jit(solution)/shard_map/ppermute | solution.py:270
  392.2 7.6 %collective-permute-done.33 = bf16[240,768]{1,0:T(8,128)(2,1)S(1)} collective-permute-done((bf16[240,768]{1,0:T(8,128)(2,1)S(1)}, bf16[240,768]{1,0:T(8,128)(2,1)S(1)}, u32[]{:S(2)}, u32[]{:S(2)}) %collective-permute-start.33) | collective-permute-done | bytes 368672 | tf_op jit(solution)/shard_map/ppermute | solution.py:270
  402.7 5.7 %collective-permute-done.43 = bf16[384,768]{1,0:T(8,128)(2,1)S(1)} collective-permute-done((bf16[384,768]{1,0:T(8,128)(2,1)S(1)}, bf16[384,768]{1,0:T(8,128)(2,1)S(1)}, u32[]{:S(2)}, u32[]{:S(2)}) %collective-permute-start.43) | collective-permute-done | bytes 589856 | tf_op jit(solution)/shard_map/ppermute | solution.py:270
  410.1 13.2 %collective-permute-done.34 = bf16[480,768]{1,0:T(8,128)(2,1)S(1)} collective-permute-done((bf16[480,768]{1,0:T(8,128)(2,1)S(1)}, bf16[480,768]{1,0:T(8,128)(2,1)S(1)}, u32[]{:S(2)}, u32[]{:S(2)}) %collective-permute-start.34) | collective-permute-done | bytes 737312 | tf_op jit(solution)/shard_map/ppermute | solution.py:270
  (426 shorter events, 202.9 us)
Async XLA Ops:
  9.6 25.7 %collective-permute-start.1 = (bf16[768,576]{0,1:T(8,128)(2,1)}, bf16[768,576]{0,1:T(8,128)(2,1)}, u32[]{:S(2)}, u32[]{:S(2)}) collective-permute-start(bf16[768,576]{0,1:T(8,128)(2,1)} %constant_dynamic-update-slice_fusion.2), channel_id=1, source_target_pairs={{0,1},{1,0},{2,3},{3,2},{4,5},{5,4},{6,7},{7,6},{8,9},{9,8},{10,11... | collective-permute-start | bytes 2654216 | tf_op jit(solution)/shard_map/ppermute | solution.py:264
  10.1 22.8 %collective-permute-start.4 = (bf16[768,576]{0,1:T(8,128)(2,1)}, bf16[768,576]{0,1:T(8,128)(2,1)}, u32[]{:S(2)}, u32[]{:S(2)}) collective-permute-start(bf16[768,576]{0,1:T(8,128)(2,1)} %constant_dynamic-update-slice_fusion.2), channel_id=1, source_target_pairs={{0,2},{1,3},{2,0},{3,1},{4,6},{5,7},{6,4},{7,5},{8,10},{9,11},{10,... | collective-permute-start | bytes 2654216 | tf_op jit(solution)/shard_map/ppermute | solution.py:267
  10.1 36.5 %collective-permute-start.3 = (bf16[192,768]{1,0:T(8,128)(2,1)}, bf16[192,768]{1,0:T(8,128)(2,1)}, u32[]{:S(2)}, u32[]{:S(2)}) collective-permute-start(bf16[192,768]{1,0:T(8,128)(2,1)} %param.26), channel_id=1, source_target_pairs={{0,1},{1,0},{2,3},{3,2},{4,5},{5,4},{6,7},{7,6},{8,9},{9,8},{10,11... | collective-permute-start | bytes 884744 | tf_op jit(solution)/shard_map/ppermute | solution.py:264
  12.6 36.8 %collective-permute-start.6 = (bf16[192,768]{1,0:T(8,128)(2,1)}, bf16[192,768]{1,0:T(8,128)(2,1)S(1)}, u32[]{:S(2)}, u32[]{:S(2)}) collective-permute-start(bf16[192,768]{1,0:T(8,128)(2,1)} %param.26), channel_id=1, source_target_pairs={{0,2},{1,3},{2,0},{3,1},{4,6},{5,7},{6,4},{7,5},{8,10},{9,11},{10,... | collective-permute-start | bytes 884744 | tf_op jit(solution)/shard_map/ppermute | solution.py:267
  17.9 46.5 %collective-permute-start.10 = (bf16[768,768]{1,0:T(8,128)(2,1)S(1)}, bf16[768,768]{1,0:T(8,128)(2,1)S(1)}, u32[]{:S(2)}, u32[]{:S(2)}) collective-permute-start(bf16[768,768]{1,0:T(8,128)(2,1)S(1)} %copy-done.22), channel_id=1, source_target_pairs={{0,2},{1,3},{2,0},{3,1},{4,6},{5,7},{6,4},{7,5},{8,10},{9,11},{10,... | collective-permute-start | bytes 3538952 | tf_op jit(solution)/shard_map/ppermute | solution.py:267
  32.9 55.8 %collective-permute-start.12 = (bf16[768,768]{1,0:T(8,128)(2,1)S(1)}, bf16[768,768]{1,0:T(8,128)(2,1)S(1)}, u32[]{:S(2)}, u32[]{:S(2)}) collective-permute-start(bf16[768,768]{1,0:T(8,128)(2,1)S(1)} %copy-done.6), channel_id=1, source_target_pairs={{0,2},{1,3},{2,0},{3,1},{4,6},{5,7},{6,4},{7,5},{8,10},{9,11},{10,... | collective-permute-start | bytes 3538952 | tf_op jit(solution)/shard_map/ppermute | solution.py:267
  35.3 53.5 %collective-permute-start.7 = (bf16[768,576]{0,1:T(8,128)(2,1)}, bf16[768,576]{0,1:T(8,128)(2,1)S(1)}, u32[]{:S(2)}, u32[]{:S(2)}) collective-permute-start(bf16[768,576]{0,1:T(8,128)(2,1)} %collective-permute-done.4), channel_id=1, source_target_pairs={{0,1},{1,0},{2,3},{3,2},{4,5},{5,4},{6,7},{7,6},{8,9},{9,8},{10,11... | collective-permute-start | bytes 2654216 | tf_op jit(solution)/shard_map/ppermute | solution.py:264
  46.6 61.6 %collective-permute-start.14 = (bf16[768,768]{1,0:T(8,128)(2,1)S(1)}, bf16[768,768]{1,0:T(8,128)(2,1)S(1)}, u32[]{:S(2)}, u32[]{:S(2)}) collective-permute-start(bf16[768,768]{1,0:T(8,128)(2,1)S(1)} %copy-done.22), channel_id=1, source_target_pairs={{0,1},{1,0},{2,3},{3,2},{4,5},{5,4},{6,7},{7,6},{8,9},{9,8},{10,11... | collective-permute-start | bytes 3538952 | tf_op jit(solution)/shard_map/ppermute | solution.py:264
  49.4 58.8 %collective-permute-start.15 = (bf16[768,768]{1,0:T(8,128)(2,1)S(1)}, bf16[768,768]{1,0:T(8,128)(2,1)S(1)}, u32[]{:S(2)}, u32[]{:S(2)}) collective-permute-start(bf16[768,768]{1,0:T(8,128)(2,1)S(1)} %copy-done.6), channel_id=1, source_target_pairs={{0,1},{1,0},{2,3},{3,2},{4,5},{5,4},{6,7},{7,6},{8,9},{9,8},{10,11... | collective-permute-start | bytes 3538952 | tf_op jit(solution)/shard_map/ppermute | solution.py:264
  64.4 30.4 %collective-permute-start.9 = (bf16[192,768]{1,0:T(8,128)(2,1)S(1)}, bf16[192,768]{1,0:T(8,128)(2,1)S(1)}, u32[]{:S(2)}, u32[]{:S(2)}) collective-permute-start(bf16[192,768]{1,0:T(8,128)(2,1)S(1)} %collective-permute-done.6), channel_id=1, source_target_pairs={{0,1},{1,0},{2,3},{3,2},{4,5},{5,4},{6,7},{7,6},{8,9},{9,8},{10,11... | collective-permute-start | bytes 884744 | tf_op jit(solution)/shard_map/ppermute | solution.py:264
  88.7 35.2 %collective-permute-start.11 = (bf16[768,768]{1,0:T(8,128)(2,1)S(1)}, bf16[768,768]{1,0:T(8,128)(2,1)S(1)}, u32[]{:S(2)}, u32[]{:S(2)}) collective-permute-start(bf16[768,768]{1,0:T(8,128)(2,1)S(1)} %collective-permute-done.10.up_ref), channel_id=1, source_target_pairs={{0,1},{1,0},{2,3},{3,2},{4,5},{5,4},{6,7},{7,6},{8,9},{9,8},{10,11... | collective-permute-start | bytes 3538952 | tf_op jit(solution)/shard_map/ppermute | solution.py:264
  88.8 35.2 %collective-permute-start.13 = (bf16[768,768]{1,0:T(8,128)(2,1)S(1)}, bf16[768,768]{1,0:T(8,128)(2,1)}, u32[]{:S(2)}, u32[]{:S(2)}) collective-permute-start(bf16[768,768]{1,0:T(8,128)(2,1)S(1)} %collective-permute-done.12.down_ref), channel_id=1, source_target_pairs={{0,1},{1,0},{2,3},{3,2},{4,5},{5,4},{6,7},{7,6},{8,9},{9,8},{10,11... | collective-permute-start | bytes 3538952 | tf_op jit(solution)/shard_map/ppermute | solution.py:264
  209.2 60.5 %collective-permute-start.35 = (bf16[768,768]{1,0:T(8,128)(2,1)}, bf16[768,768]{1,0:T(8,128)(2,1)}, u32[]{:S(2)}, u32[]{:S(2)}) collective-permute-start(bf16[768,768]{1,0:T(8,128)(2,1)} %convolution_convert_fusion.2), channel_id=1, source_target_pairs={{0,1},{1,0},{2,3},{3,2},{4,5},{5,4},{6,7},{7,6},{8,9},{9,8},{10,11... | collective-permute-start | bytes 3538952 | tf_op jit(solution)/shard_map/ppermute | solution.py:264
  213.0 34.0 %collective-permute-start.36 = (bf16[768,768]{1,0:T(8,128)(2,1)}, bf16[768,768]{1,0:T(8,128)(2,1)}, u32[]{:S(2)}, u32[]{:S(2)}) collective-permute-start(bf16[768,768]{1,0:T(8,128)(2,1)} %convolution_convert_fusion), channel_id=1, source_target_pairs={{0,1},{1,0},{2,3},{3,2},{4,5},{5,4},{6,7},{7,6},{8,9},{9,8},{10,11... | collective-permute-start | bytes 3538952 | tf_op jit(solution)/shard_map/ppermute | solution.py:264
  216.5 32.4 %collective-permute-start.27 = (bf16[960,768]{1,0:T(8,128)(2,1)}, bf16[960,768]{1,0:T(8,128)(2,1)}, u32[]{:S(2)}, u32[]{:S(2)}) collective-permute-start(bf16[960,768]{1,0:T(8,128)(2,1)} %pad_maximum_fusion.1), channel_id=1, source_target_pairs={{0,1},{1,0},{2,3},{3,2},{4,5},{5,4},{6,7},{7,6},{8,9},{9,8},{10,11... | collective-permute-start | bytes 4423688 | tf_op jit(solution)/shard_map/ppermute | solution.py:264
  244.4 24.7 %collective-permute-start.19 = (bf16[768,640]{0,1:T(8,128)(2,1)S(1)}, bf16[768,640]{0,1:T(8,128)(2,1)S(1)}, u32[]{:S(2)}, u32[]{:S(2)}) collective-permute-start(bf16[768,640]{0,1:T(8,128)(2,1)S(1)} %add_convert_fusion.7), channel_id=1, source_target_pairs={{0,2},{1,3},{2,0},{3,1},{4,6},{5,7},{6,4},{7,5},{8,10},{9,11},{10,... | collective-permute-start | bytes 2949128 | tf_op jit(solution)/shard_map/ppermute | solution.py:267
  244.9 28.3 %collective-permute-start.26 = (bf16[960,768]{1,0:T(8,128)(2,1)S(1)}, bf16[960,768]{1,0:T(8,128)(2,1)S(1)}, u32[]{:S(2)}, u32[]{:S(2)}) collective-permute-start(bf16[960,768]{1,0:T(8,128)(2,1)S(1)} %pad_maximum_fusion), channel_id=1, source_target_pairs={{0,1},{1,0},{2,3},{3,2},{4,5},{5,4},{6,7},{7,6},{8,9},{9,8},{10,11... | collective-permute-start | bytes 4423688 | tf_op jit(solution)/shard_map/ppermute | solution.py:264
  247.0 80.9 %collective-permute-start.16 = (bf16[256,768]{1,0:T(8,128)(2,1)S(1)}, bf16[256,768]{1,0:T(8,128)(2,1)}, u32[]{:S(2)}, u32[]{:S(2)}) collective-permute-start(bf16[256,768]{1,0:T(8,128)(2,1)S(1)} %slice.203), channel_id=1, source_target_pairs={{0,1},{1,0},{2,3},{3,2},{4,5},{5,4},{6,7},{7,6},{8,9},{9,8},{10,11... | collective-permute-start | bytes 1179656 | tf_op jit(solution)/shard_map/ppermute | solution.py:264
  248.9 45.5 %collective-permute-start.37 = (bf16[768,768]{1,0:T(8,128)(2,1)S(1)}, bf16[768,768]{1,0:T(8,128)(2,1)S(1)}, u32[]{:S(2)}, u32[]{:S(2)}) collective-permute-start(bf16[768,768]{1,0:T(8,128)(2,1)S(1)} %add_convert_fusion.4), channel_id=1, source_target_pairs={{0,2},{1,3},{2,0},{3,1},{4,6},{5,7},{6,4},{7,5},{8,10},{9,11},{10,... | collective-permute-start | bytes 3538952 | tf_op jit(solution)/shard_map/ppermute | solution.py:267
  269.1 56.0 %collective-permute-start.28 = (bf16[960,768]{1,0:T(8,128)(2,1)S(1)}, bf16[960,768]{1,0:T(8,128)(2,1)S(1)}, u32[]{:S(2)}, u32[]{:S(2)}) collective-permute-start(bf16[960,768]{1,0:T(8,128)(2,1)S(1)} %add_convert_fusion.1), channel_id=1, source_target_pairs={{0,2},{1,3},{2,0},{3,1},{4,6},{5,7},{6,4},{7,5},{8,10},{9,11},{10,... | collective-permute-start | bytes 4423688 | tf_op jit(solution)/shard_map/ppermute | solution.py:267
  295.5 36.3 %collective-permute-start.38 = (bf16[384,768]{1,0:T(8,128)(2,1)}, bf16[384,768]{1,0:T(8,128)(2,1)}, u32[]{:S(2)}, u32[]{:S(2)}) collective-permute-start(bf16[384,768]{1,0:T(8,128)(2,1)} %constant_dynamic-slice_fusion.2), channel_id=1, source_target_pairs={{0,4},{4,0},{8,12},{12,8},{16,20},{20,16},{24,28},{28,24},{1,5},{5... | collective-permute-start | bytes 1769480 | tf_op jit(solution)/shard_map/ppermute | solution.py:270
  298.0 30.9 %collective-permute-start.22 = (bf16[96,640]{0,1:T(8,128)(2,1)}, bf16[96,640]{0,1:T(8,128)(2,1)S(1)}, u32[]{:S(2)}, u32[]{:S(2)}) collective-permute-start(bf16[96,640]{0,1:T(8,128)(2,1)} %constant_dynamic-slice_fusion.6), channel_id=1, source_target_pairs={{0,16},{4,20},{8,24},{12,28},{16,0},{20,4},{24,8},{28,12},{1,17},{... | collective-permute-start | bytes 368648 | tf_op jit(solution)/shard_map/ppermute | solution.py:270
  351.6 34.2 %collective-permute-start.25 = (bf16[384,640]{0,1:T(8,128)(2,1)S(1)}, bf16[384,640]{0,1:T(8,128)(2,1)S(1)}, u32[]{:S(2)}, u32[]{:S(2)}) collective-permute-start(bf16[384,640]{0,1:T(8,128)(2,1)S(1)} %maximum_select_fusion.5), channel_id=1, source_target_pairs={{0,4},{4,0},{8,12},{12,8},{16,20},{20,16},{24,28},{28,24},{1,5},{5... | collective-permute-start | bytes 1474568 | tf_op jit(solution)/shard_map/ppermute | solution.py:270
  400.1 23.1 %collective-permute-start.34 = (bf16[480,768]{1,0:T(8,128)(2,1)S(1)}, bf16[480,768]{1,0:T(8,128)(2,1)S(1)}, u32[]{:S(2)}, u32[]{:S(2)}) collective-permute-start(bf16[480,768]{1,0:T(8,128)(2,1)S(1)} %maximum_select_fusion.3), channel_id=1, source_target_pairs={{0,4},{4,0},{8,12},{12,8},{16,20},{20,16},{24,28},{28,24},{1,5},{5... | collective-permute-start | bytes 2211848 | tf_op jit(solution)/shard_map/ppermute | solution.py:270
  (112 other events, 826.5 us)
